TPU v7x, 32 devices: a whole 2x2x4 slice. The times are simulated.
32 devices in a mesh: grp: 2 (over x), chi: 16 (over z, y, core).
Axes of the slice: x: 2, y: 2, z: 4, core: 2. Of those that a mesh axis runs over, the one named last changes fastest.
Arguments:
- edge: bfloat16 [768, 32, 384], P(('grp', 'chi')), parts along dimension 0, may hold values from -6 to 6
- proj_upper: bfloat16 [768, 32, 384], P(('grp', 'chi')), parts along dimension 0, may hold values from -0.3125 to 0.3125
- proj_lower: bfloat16 [768, 32, 384], P(('grp', 'chi')), parts along dimension 0, may hold values from -0.3125 to 0.3125
- site: bfloat16 [2048, 1024], P('grp'), parts along dimension 0, may hold values from -0.1875 to 0.1875
- chi_charge: int32 [768], P('grp'), parts along dimension 0, may hold values from 0 to 7
- bond_charge: int32 [64], P('grp'), parts along dimension 0, may hold values from 0 to 3
- new_charge: int32 [768], P('grp'), parts along dimension 0, may hold values from 0 to 10
Outputs:
- new_edge: bfloat16 [768, 32, 384], P(('grp', 'chi')), parts along dimension 0
There are 2 independent parts, one for each index of `grp`. A program takes and returns all parts, laid end to end along the dimension named above; each array names one. Nothing has to cross between parts.
All inputs are finite; a program needn't handle non-finite values. Where the computation divides by a largest or mean magnitude, that divisor is 1e-20 or more.
Results may differ from a plain program's by a relative error of at most 0.0059.
Values may be sent and summed in bfloat16 or wider, within the bound.
A program may use at most 320 MiB of HBM per device.

v0:
```python
import jax
import jax.numpy as jnp
from jax import lax
from jax.sharding import PartitionSpec as P


def masked_rows(piece, charges, bond_charge, new_charge):
    keep = charges[:, None, None] + bond_charge[None, :, None] == new_charge[None, None, :]
    return jnp.where(keep, piece, jnp.zeros_like(piece))


def local(edge, proj_upper, proj_lower, site, chi_charge, bond_charge, new_charge):
    rows = edge.shape[0]
    kdim = bond_charge.shape[0]
    width = chi_charge.shape[0]
    mine = lax.axis_index("chi") * rows
    pair = (bond_charge[:, None] + bond_charge[None, :]).reshape(kdim * kdim)
    block = jnp.where(pair[:, None] == pair[None, :], site, jnp.zeros_like(site))
    piece = lax.all_gather(proj_upper, "chi", axis=0, tiled=True)
    count = piece.shape[0]
    masked = masked_rows(piece, chi_charge, bond_charge, new_charge)
    half = jnp.dot(
        edge.reshape(rows * kdim, count),
        masked.reshape(count, kdim * width),
        preferred_element_type=jnp.float32,
    )
    half = half.astype(jnp.bfloat16).reshape(rows, kdim * kdim, width)
    grown = jnp.einsum("bxc,xy->byc", half, block, preferred_element_type=jnp.float32).astype(
        jnp.bfloat16
    )
    grown = grown.reshape(rows, kdim, kdim, width)
    own_charges = lax.dynamic_slice_in_dim(chi_charge, mine, rows)
    lower = masked_rows(proj_lower, own_charges, bond_charge, new_charge)
    raw = lax.psum_scatter(
        jnp.einsum("brdc,bde->cre", grown, lower, preferred_element_type=jnp.float32),
        "chi",
        scatter_dimension=0,
        tiled=True,
    )
    largest = lax.pmax(jnp.max(jnp.abs(raw)), "chi")
    return (raw / (largest + 1e-06)).astype(jnp.bfloat16)


def solution(mesh):
    placed = (
        P(("grp", "chi"), None, None),
        P(("grp", "chi"), None, None),
        P(("grp", "chi"), None, None),
        P("grp", None),
        P("grp"),
        P("grp"),
        P("grp"),
    )
    return jax.shard_map(
        local, mesh=mesh, in_specs=placed, out_specs=P(("grp", "chi"), None, None), check_vma=False
    )
```

profile of v0, /device:TPU:0, one launch (start us, length us, event | category | flops | bytes accessed | tf_op | source)
XLA Modules:
  0.0 488.2 jit_solution(14152442403010330114)
XLA Ops:
  6.5 0.0 copy-start
  6.5 0.7 all-gather.2.cloned.1.call-update
  7.3 0.0 reduce-scatter.2.cloned.1.call-start
  7.3 0.8 broadcast_add_fusion.1
  8.1 0.1 add.75
  8.2 0.8 dynamic_slice.3
  8.9 0.7 broadcast_add_fusion.2
  9.7 0.8 broadcast_add_fusion
  10.5 83.3 %all-gather.2.cloned.1.call-done = bf16[384,32,384]{2,1,0:T(8,128)(2,1)} async-done(((bf16[24,32,384]{2,1,0:T(8,128)(2,1)}), bf16[384,32,384]{2,1,0:T(8,128)(2,1)}) %all-gather.2.cloned.1.call-update) | async-done | bytes 9437200 | tf_op jit(solution)/shard_map/all_gather | solution.py:19
  93.8 10.4 %compare_select_fusion = bf16[384,32,384]{2,1,0:T(8,128)(2,1)} fusion(bf16[384,32,384]{2,1,0:T(8,128)(2,1)} %all-gather.2.cloned.1.call-done, s32[384]{0:T(512)} %param.13, s32[384,32]{1,0:T(8,128)S(1)} %broadcast_add_fusion), kind=kLoop, calls=%fused_computation.1 | loop fusion | flops 9437184 | bytes 18925056 | tf_op jit(solution)/shard_map/jit(_where)/select_n | solution.py:9
  104.3 11.9 %copy.22 = bf16[48,8,32,384]{3,1,2,0:T(8,128)(2,1)} copy(bf16[48,8,32,384]{3,2,1,0:T(8,128)(2,1)} %bitcast.28) | data formatting | bytes 18874368
  116.2 16.9 %fusion = bf16[768,12288]{0,1:T(8,128)(2,1)} fusion(bf16[384,12288]{1,0:T(8,128)(2,1)} %bitcast.29, bf16[768,384]{1,0:T(8,128)(2,1)S(1)} %bitcast.27), kind=kOutput, calls=%fused_computation.2 | convolution fusion | flops 7257194496 | bytes 28901376 | tf_op jit(solution)/shard_map/dot_general | solution.py:22
  133.1 24.6 %copy.15 = bf16[768,12288]{1,0:T(8,128)(2,1)} copy(bf16[768,12288]{0,1:T(8,128)(2,1)} %fusion) | data formatting | bytes 37748736 | tf_op jit(solution)/shard_map/convert_element_type | solution.py:27
  157.7 27.1 %reshape.107 = bf16[24,1024,384]{2,1,0:T(8,128)(2,1)} reshape(bf16[768,12288]{1,0:T(8,128)(2,1)} %copy.15) | data formatting | bytes 37748736 | tf_op jit(solution)/shard_map/reshape | solution.py:27
  184.8 0.0 copy-done.3
  184.8 29.6 %convolution_convert_fusion.1 = bf16[1024,24,384]{2,0,1:T(8,128)(2,1)} fusion(bf16[24,1024,384]{2,1,0:T(8,128)(2,1)} %reshape.107, bf16[1024,1024]{1,0:T(8,128)(2,1)S(1)} %copy-done.3, s32[1024]{0:T(1024)S(1)} %add.75), kind=kOutput, calls=%fused_computation.3 | convolution fusion | flops 19338887168 | bytes 39849984 | tf_op jit(solution)/shard_map/bxc,xy->byc/dot_general | solution.py:28
  214.5 0.0 copy-done.2
  214.5 17.8 %convolution_bitcast_fusion = f32[384,32,384]{0,2,1:T(8,128)} fusion(bf16[24,32,32,384]{3,2,1,0:T(8,128)(2,1)} %bitcast.30, bf16[24,32,384]{2,1,0:T(8,128)(2,1)S(1)} %copy-done.4, s32[384]{0:T(512)S(1)} %copy-done.2, s32[24,32]{1,0:T(8,128)S(1)} %broadcast_add_fusion.2), kind=kOutput, calls=%fused_computation.4 | convolution fusion | flops 7248347136 | bytes 38343168 | tf_op jit(solution)/shard_map/brdc,bde->cre/dot_general | solution.py:35
  232.3 19.0 %copy.18 = f32[384,32,384]{2,1,0:T(8,128)} copy(f32[384,32,384]{0,2,1:T(8,128)} %convolution_bitcast_fusion) | data formatting | bytes 37748736 | tf_op jit(solution)/shard_map/brdc,bde->cre/transpose | solution.py:35
  251.2 0.0 reduce-scatter.2.cloned.1.call-update
  251.3 193.2 %reduce-scatter.2.cloned.1.call-done = f32[24,32,384]{2,1,0:T(8,128)} async-done(((f32[384,32,384]{2,1,0:T(8,128)}), f32[24,32,384]{2,1,0:T(8,128)}) %reduce-scatter.2.cloned.1.call-update) | async-done | bytes 1179664 | tf_op jit(solution)/shard_map/reduce_scatter | solution.py:34
  444.5 2.0 abs_reduce_fusion
  446.4 32.1 %pmax.7 = f32[]{:T(128)} all-reduce(f32[]{:T(128)} %abs_reduce_fusion), channel_id=1, replica_groups=mesh['grp'=2,'chi'=16] {'chi'}, use_global_device_ids=true, to_apply=%region_2.3 | all-reduce | flops 1 | bytes 8 | tf_op jit(solution)/shard_map/pmax | solution.py:40
  479.2 2.2 divide_convert_fusion
  (8 shorter events, 0.0 us)
Async XLA Ops:
  6.5 109.6 %copy-start = (bf16[24,32,384]{2,1,0:T(8,128)(2,1)S(1)}, bf16[24,32,384]{2,1,0:T(8,128)(2,1)}, u32[]{:S(2)}) copy-start(bf16[24,32,384]{2,1,0:T(8,128)(2,1)} %param.7) | copy-start | bytes 1769476
  6.5 87.3 %all-gather.2.cloned.1.call-start = ((), (), s32[]{:S(2)}) async-start(), calls=%async_computation.1 | async-start | bytes 10027008 | tf_op jit(solution)/shard_map/all_gather | solution.py:19
  7.3 437.2 %reduce-scatter.2.cloned.1.call-start = ((), (), s32[]{:S(2)}) async-start(), calls=%async_computation.2 | async-start | bytes 20054016 | tf_op jit(solution)/shard_map/reduce_scatter | solution.py:34
  157.7 27.1 %copy-start.3 = (bf16[1024,1024]{1,0:T(8,128)(2,1)S(1)}, bf16[1024,1024]{1,0:T(8,128)(2,1)}, u32[]{:S(2)}) copy-start(bf16[1024,1024]{1,0:T(8,128)(2,1)} %param.10) | copy-start | bytes 6291460
  184.8 29.6 %copy-start.2 = (s32[384]{0:T(512)S(1)}, s32[384]{0:T(512)}, u32[]{:S(2)}) copy-start(s32[384]{0:T(512)} %param.13) | copy-start | bytes 4612
  184.8 29.6 %copy-start.4 = (bf16[24,32,384]{2,1,0:T(8,128)(2,1)S(1)}, bf16[24,32,384]{2,1,0:T(8,128)(2,1)}, u32[]{:S(2)}) copy-start(bf16[24,32,384]{2,1,0:T(8,128)(2,1)} %param.9) | copy-start | bytes 1769476
  251.2 230.2 %copy-start.1 = (bf16[24,32,384]{2,1,0:T(8,128)(2,1)S(1)}, bf16[24,32,384]{2,1,0:T(8,128)(2,1)}, u32[]{:S(2)}) copy-start(bf16[24,32,384]{2,1,0:T(8,128)(2,1)} %param.7) | copy-start | bytes 1769476
Sparse Core Ops, SparseCore 0:
  9.6 84.1 all-gather.1
  251.4 193.0 reduce-scatter.1
where the time goes:
time: 490 us; the launch traced here: 488 us
  waiting for transfers between devices  277 us (57%)
  local copies, waits for them, and re-layouts  83.5 us (17%)
  matrix products  64.3 us (13%)
  blocking collectives  32.1 us (7%)
  other arithmetic  16.9 us (3%)
  between operations  14.1 us (3%)
    reduce_scatter x1, waiting for transfers between devices, local(): lax.psum_scatter(jnp.einsum('brdc,bde->cre', grown, lower, preferred_elem...  193 us
    all_gather x1, waiting for transfers between devices, local(): piece = lax.all_gather(proj_upper, 'chi', axis=0, tiled=True)  83.3 us
    pmax x1, blocking collectives, local(): largest = lax.pmax(jnp.max(jnp.abs(raw)), 'chi')  32.1 us
    dot_general x1, matrix products, local(): jnp.einsum('bxc,xy->byc', half, block, preferred_element_type=jnp.float32)  29.6 us
    reshape x1, local copies, waits for them, and re-layouts, local(): half = half.astype(jnp.bfloat16).reshape(rows, kdim * kdim, width)  27.1 us
    convert_element_type x1, local copies, waits for them, and re-layouts, local(): half = half.astype(jnp.bfloat16).reshape(rows, kdim * kdim, width)  24.6 us
    transpose x1, local copies, waits for them, and re-layouts, local(): jnp.einsum('brdc,bde->cre', grown, lower, preferred_element_type=jnp.floa...  19 us
    dot_general x1, matrix products, local(): jnp.einsum('brdc,bde->cre', grown, lower, preferred_element_type=jnp.floa...  17.8 us
  transfers between devices with their start and end apart: 2, of which 2 were waited for; matrix products, arithmetic and copies ran while one was open for 1% of the time, Pallas kernels for 0%

commit v1 on v0

v1 whole, which is shorter than its diff:
```python
import functools

import jax
import jax.numpy as jnp
from jax import lax
from jax.experimental import pallas as pl
from jax.experimental.pallas import tpu as pltpu
from jax.sharding import PartitionSpec as P

BF = jnp.bfloat16
F32 = jnp.float32
EDGE, LOWER = 0, 1
RIGHT, LEFT, ACROSS, SIBLING = 0, 1, 2, 3
MESH = pl.DeviceIdType.MESH


def masked_rows(piece, charges, bond_charge, new_charge):
    keep = charges[:, None, None] + bond_charge[None, :, None] == new_charge[None, None, :]
    return jnp.where(keep, piece, jnp.zeros_like(piece))


def plain(edge, proj_upper, proj_lower, site, chi_charge, bond_charge, new_charge):
    rows = edge.shape[0]
    kdim = bond_charge.shape[0]
    width = chi_charge.shape[0]
    mine = lax.axis_index("chi") * rows
    pair = (bond_charge[:, None] + bond_charge[None, :]).reshape(kdim * kdim)
    block = jnp.where(pair[:, None] == pair[None, :], site, jnp.zeros_like(site))
    piece = lax.all_gather(proj_upper, "chi", axis=0, tiled=True)
    count = piece.shape[0]
    masked = masked_rows(piece, chi_charge, bond_charge, new_charge)
    half = jnp.dot(
        edge.reshape(rows * kdim, count),
        masked.reshape(count, kdim * width),
        preferred_element_type=F32,
    )
    half = half.astype(BF).reshape(rows, kdim * kdim, width)
    grown = jnp.einsum("bxc,xy->byc", half, block, preferred_element_type=F32).astype(BF)
    grown = grown.reshape(rows, kdim, kdim, width)
    own_charges = lax.dynamic_slice_in_dim(chi_charge, mine, rows)
    lower = masked_rows(proj_lower, own_charges, bond_charge, new_charge)
    raw = lax.psum_scatter(
        jnp.einsum("brdc,bde->cre", grown, lower, preferred_element_type=F32),
        "chi",
        scatter_dimension=0,
        tiled=True,
    )
    largest = lax.pmax(jnp.max(jnp.abs(raw)), "chi")
    return (raw / (largest + 1e-06)).astype(BF)


def kernel(
    n, depth, edge_ref, lower_ref, upper_ref, block_ref, out_ref,
    edge_all, lower_all, swap, up_rx, up_wide, up_t, state, total, peaks,
    swap_send, swap_recv, up_send, up_recv, blk_send, blk_recv, peak_send, peak_recv,
):
    kdim, rows, width = edge_ref.shape
    part = kdim // 2
    wide = 2 * rows
    chips = n // 2
    pairs = kdim * kdim
    me = lax.axis_index("chi")
    core = lax.rem(me, 2)
    chip = me // 2
    y = lax.rem(chip, 2)
    z = chip // 2
    sibling = me + 1 - 2 * core

    barrier = pltpu.get_barrier_semaphore()

    def greet(j, carry):
        pl.semaphore_signal(barrier, inc=1, device_id={"chi": lax.rem(me + j, n)}, device_id_type=MESH)
        return carry

    lax.fori_loop(1, n, greet, 0)
    pl.semaphore_wait(barrier, n - 1)

    ins = (edge_ref, lower_ref)
    fulls = (edge_all, lower_all)

    def swap_copy(which):
        return pltpu.make_async_remote_copy(
            src_ref=ins[which].at[pl.ds(part * (1 - core), part)],
            dst_ref=swap.at[which],
            send_sem=swap_send.at[which],
            recv_sem=swap_recv.at[which],
            device_id={"chi": sibling},
            device_id_type=MESH,
        )

    def block_copy(which, q, side, way, target):
        here = fulls[which].at[q, pl.ds(part * side, part)]
        return pltpu.make_async_remote_copy(
            src_ref=here,
            dst_ref=here,
            send_sem=blk_send.at[which, q, way],
            recv_sem=blk_recv.at[which, q, side],
            device_id={"chi": target},
            device_id_type=MESH,
        )

    def ways(which, q):
        targets = (me + 4, me - 4, me + 2 - 4 * y, sibling)

        def send(way):
            block_copy(which, q, core, way, targets[way]).start()

        def leave(way):
            block_copy(which, q, core, way, targets[way]).wait_send()

        return send, leave

    def arrived(which, q, side):
        block_copy(which, q, side, SIBLING, sibling).wait_recv()

    def up_copy(j):
        to = lax.rem(me + j, n)
        return pltpu.make_async_remote_copy(
            src_ref=upper_ref.at[to],
            dst_ref=up_rx.at[me],
            send_sem=up_send.at[j],
            recv_sem=up_recv.at[j],
            device_id={"chi": to},
            device_id_type=MESH,
        )

    def each(lo, hi, act):
        def body(j, carry):
            act(j)
            return carry

        lax.fori_loop(lo, hi, body, 0)

    def join(which):
        swap_copy(which).wait_recv()

        def body(j):
            own = ins[which][part * core + j].astype(F32)
            other = swap[which, j].astype(F32)
            first = jnp.where(core == 0, own, other)
            second = jnp.where(core == 0, other, own)
            fulls[which][chip, part * core + j] = jnp.concatenate([first, second], axis=0).astype(BF)

        each(0, part, body)

    def open_ring(which):
        send, _ = ways(which, chip)
        pl.when(z < depth - 1)(lambda: send(RIGHT))
        pl.when(z > 0)(lambda: send(LEFT))
        send(ACROSS)
        send(SIBLING)

    def along(which, s):
        @pl.when(z - s >= 0)
        def _():
            q = chip - 2 * s
            arrived(which, q, core)
            send, _ = ways(which, q)
            pl.when(z < depth - 1)(lambda: send(RIGHT))
            send(ACROSS)
            send(SIBLING)

        @pl.when(z + s < depth)
        def _():
            q = chip + 2 * s
            arrived(which, q, core)
            send, _ = ways(which, q)
            pl.when(z > 0)(lambda: send(LEFT))
            send(ACROSS)
            send(SIBLING)

    def beside(which, s):
        other = chip + 1 - 2 * y
        for sign in (-1, 1) if s else (1,):
            @pl.when(jnp.logical_and(z + sign * s >= 0, z + sign * s < depth))
            def _():
                q = other + 2 * sign * s
                arrived(which, q, core)
                block_copy(which, q, core, SIBLING, sibling).start()

    def close_ring(which):
        each(0, chips, lambda q: arrived(which, q, 1 - core))

    def sent(which):
        def body(q):
            _, leave = ways(which, q)
            column = q // 2
            mine = lax.rem(q, 2) == y
            pl.when(jnp.logical_and(mine, jnp.logical_and(column <= z, z < depth - 1)))(lambda: leave(RIGHT))
            pl.when(jnp.logical_and(mine, jnp.logical_and(column >= z, z > 0)))(lambda: leave(LEFT))
            pl.when(mine)(lambda: leave(ACROSS))
            leave(SIBLING)

        each(0, chips, body)

    swap_copy(EDGE).start()
    swap_copy(LOWER).start()
    join(EDGE)
    open_ring(EDGE)
    each(1, n, lambda j: up_copy(j).start())
    join(LOWER)
    up_rx[me] = upper_ref[me]
    along(EDGE, 1)
    beside(EDGE, 0)
    each(1, n, lambda j: up_copy(j).wait_recv())
    for j in range(n):
        up_wide[j * rows:(j + 1) * rows, :] = up_rx[j].astype(F32)
    up_t[...] = up_wide[...].T.astype(BF)
    along(EDGE, 2)
    beside(EDGE, 1)
    along(EDGE, 3)
    open_ring(LOWER)
    beside(EDGE, 2)
    beside(EDGE, 3)
    close_ring(EDGE)

    def first(j):
        right = edge_all[:, j].reshape(width, width)
        half = lax.dot_general(up_t[...], right, (((1,), (1,)), ((), ())), preferred_element_type=F32)
        at = pl.multiple_of(j * kdim, kdim)
        state[1:rows + 1, pl.ds(at, kdim), :] = half.astype(BF).reshape(rows, kdim, width)

    each(0, kdim, first)

    def second(j):
        c = 2 * j
        right = jnp.concatenate([state[c + 1], state[c + 2]], axis=1)
        grown = jnp.dot(block_ref[...], right, preferred_element_type=F32).astype(BF)
        state[c] = grown[:, :width]
        state[c + 1] = grown[:, width:]

    third_of = rows // 6
    along(LOWER, 1)
    beside(LOWER, 0)
    each(0, third_of, second)
    along(LOWER, 2)
    beside(LOWER, 1)
    each(third_of, 2 * third_of, second)
    along(LOWER, 3)
    beside(LOWER, 2)
    each(2 * third_of, rows // 2, second)
    beside(LOWER, 3)
    close_ring(LOWER)

    total[...] = jnp.zeros_like(total)

    def third(j):
        at = pl.multiple_of(2 * j * kdim, 2 * kdim)
        left = jnp.concatenate(
            [
                state[0:rows, pl.ds(at, kdim), :].reshape(rows * kdim, width),
                state[0:rows, pl.ds(at + kdim, kdim), :].reshape(rows * kdim, width),
            ],
            axis=1,
        )
        right = jnp.concatenate(
            [lower_all[:, 2 * j].reshape(width, width), lower_all[:, 2 * j + 1].reshape(width, width)], axis=0
        )
        total[...] += jnp.dot(left, right, preferred_element_type=F32)

    each(0, kdim // 2, third)

    peaks[me] = jnp.full(peaks.shape[1:], jnp.max(jnp.abs(total[...])), F32)

    def peak_copy(j):
        return pltpu.make_async_remote_copy(
            src_ref=peaks.at[me],
            dst_ref=peaks.at[me],
            send_sem=peak_send.at[j],
            recv_sem=peak_recv.at[j],
            device_id={"chi": lax.rem(me + j, n)},
            device_id_type=MESH,
        )

    each(1, n, lambda j: peak_copy(j).start())
    each(0, 2, lambda w: pltpu.make_async_remote_copy(
        src_ref=edge_ref.at[pl.ds(0, part)], dst_ref=swap.at[w], send_sem=swap_send.at[w],
        recv_sem=swap_recv.at[w], device_id={"chi": sibling}, device_id_type=MESH).wait_send())
    each(1, n, lambda j: up_copy(j).wait_send())
    sent(EDGE)
    sent(LOWER)
    each(1, n, lambda j: peak_copy(j).wait_recv())
    each(1, n, lambda j: peak_copy(j).wait_send())
    largest = jnp.max(peaks[...])
    out_ref[...] = (total[...] / (largest + 1e-06)).astype(BF)


def fused(n, edge, proj_upper, proj_lower, site, chi_charge, bond_charge, new_charge):
    rows, kdim, width = edge.shape
    mine = lax.axis_index("chi") * rows
    own_charges = lax.dynamic_slice_in_dim(chi_charge, mine, rows)
    upper = masked_rows(proj_upper, own_charges, bond_charge, new_charge)
    lower = masked_rows(proj_lower, own_charges, bond_charge, new_charge)
    upper = upper.reshape(rows, kdim, n, rows).transpose(2, 0, 3, 1).reshape(n, rows, rows * kdim)
    pair = (bond_charge[:, None] + bond_charge[None, :]).reshape(kdim * kdim)
    block = jnp.where(pair[:, None] == pair[None, :], site, jnp.zeros_like(site))
    block = block.reshape(kdim * kdim, kdim, kdim).transpose(2, 1, 0).reshape(kdim * kdim, kdim * kdim)
    chips = n // 2
    part = kdim // 2
    dma = pltpu.SemaphoreType.DMA
    vmem = pl.BlockSpec(memory_space=pltpu.VMEM)
    out = pl.pallas_call(
        functools.partial(kernel, n, chips // 2),
        out_shape=jax.ShapeDtypeStruct((rows * kdim, width), BF),
        in_specs=[vmem] * 4,
        out_specs=vmem,
        scratch_shapes=[
            pltpu.VMEM((chips, kdim, 2 * rows, width), BF),
            pltpu.VMEM((chips, kdim, 2 * rows, width), BF),
            pltpu.VMEM((2, part, rows, width), BF),
            pltpu.VMEM((n, rows, rows * kdim), BF),
            pltpu.VMEM((width, rows * kdim), F32),
            pltpu.VMEM((rows * kdim, width), BF),
            pltpu.VMEM((rows + 1, kdim * kdim, width), BF),
            pltpu.VMEM((rows * kdim, width), F32),
            pltpu.VMEM((n, 8, 128), F32),
            dma((2,)), dma((2,)),
            dma((n,)), dma((n,)),
            dma((2, chips, 4)), dma((2, chips, 2)),
            dma((n,)), dma((n,)),
        ],
        compiler_params=pltpu.CompilerParams(
            collective_id=0, has_side_effects=True, vmem_limit_bytes=63 * 1024 * 1024
        ),
        name="edge_update",
    )(edge.transpose(1, 0, 2), lower.transpose(1, 0, 2), upper, block)
    return out.reshape(rows, kdim, width)


def solution(mesh):
    n = mesh.shape["chi"]

    def local(edge, *rest):
        rows, kdim, width = edge.shape
        if n == 16 and rows % 8 == 0 and rows % 6 == 0 and kdim % 32 == 0 and width % 128 == 0:
            return fused(n, edge, *rest)
        return plain(edge, *rest)

    placed = (
        P(("grp", "chi"), None, None),
        P(("grp", "chi"), None, None),
        P(("grp", "chi"), None, None),
        P("grp", None),
        P("grp"),
        P("grp"),
        P("grp"),
    )
    return jax.shard_map(
        local, mesh=mesh, in_specs=placed, out_specs=P(("grp", "chi"), None, None), check_vma=False
    )
```

time: 490 us -> 184 us (0.38)
  waiting for transfers between devices: 277 us -> 0 us
  Pallas kernels: 0 us -> 158 us
  matrix products: 64.3 us -> 0 us
  local copies, waits for them, and re-layouts: 83.5 us -> 21.9 us
  blocking collectives: 32.1 us -> 0 us
  between operations: 14.1 us -> 0.05 us
  other arithmetic: 16.9 us -> 4.42 us
    reduce_scatter x1 -> x0, waiting for transfers between devices: 193 us -> none  [local(): lax.psum_scatter(jnp.einsum('brdc,bde->cre', grown, lower, preferred_elem...]
    pallas_call x0 -> x1, Pallas kernels: none -> 158 us  [fused(): pl.pallas_call(functools.partial(kernel, n, chips // 2), out_shape=jax.Sh...]
    all_gather x1 -> x0, waiting for transfers between devices: 83.3 us -> none  [local(): piece = lax.all_gather(proj_upper, 'chi', axis=0, tiled=True)]
    dot_general x3 -> x0, matrix products: 64.3 us -> none  [the longest x1 29.6 us: local(): jnp.einsum('bxc,xy->byc', half, block, preferred_element_type=jnp.float32)]
    pmax x1 -> x0, blocking collectives: 32.1 us -> none  [local(): largest = lax.pmax(jnp.max(jnp.abs(raw)), 'chi')]
    convert_element_type x1 -> x0, local copies, waits for them, and re-layouts: 24.6 us -> none  [local(): half = half.astype(jnp.bfloat16).reshape(rows, kdim * kdim, width)]
    reshape x1 -> x2, local copies, waits for them, and re-layouts: 27.1 us -> 9.33 us  [fused(): upper.reshape(rows, kdim, n, rows).transpose(2, 0, 3, 1)]
    transpose x1 -> x2, local copies, waits for them, and re-layouts: 19 us -> 6.08 us  [the longest x1 3.6 us: fused(): upper.reshape(rows, kdim, n, rows).transpose(2, 0, 3, 1)]
  transfers between devices with their start and end apart: 2 -> 0, of which waited for: 2 -> 0; matrix products, arithmetic and copies ran while one was open for 1% -> 0% of each run, Pallas kernels for 0% -> 0%
where the time goes in v1:
time: 184 us
  Pallas kernels  158 us (86%)
  local copies, waits for them, and re-layouts  21.9 us (12%)
  other arithmetic  4.42 us (2%)
    pallas_call x1, Pallas kernels, fused(): pl.pallas_call(functools.partial(kernel, n, chips // 2), out_shape=jax.Sh...  158 us
    reshape x2, local copies, waits for them, and re-layouts, fused(): upper.reshape(rows, kdim, n, rows).transpose(2, 0, 3, 1)  9.33 us
    unnamed x4, local copies, waits for them, and re-layouts  4.81 us

profile of v1, /device:TPU:0, one launch (start us, length us, event | category | flops | bytes accessed | tf_op | source)
XLA Modules:
  0.0 184.0 jit_solution(11416614549027149688)
XLA Ops:
  0.0 0.8 dynamic_slice.3
  0.8 0.7 broadcast_add_fusion.1
  1.5 3.1 %compare_select_fusion.1 = (bf16[24,32,384]{2,0,1:T(8,128)(2,1)S(1)}, bf16[32,24,384]{2,1,0:T(8,128)(2,1)}, bf16[32,24,384]{2,1,0:T(8,128)(2,1)}) fusion(bf16[24,32,384]{2,1,0:T(8,128)(2,1)} %param.8, s32[384]{0:T(512)} %param.13, s32[24,32]{0,1:T(8,128)S(1)} %broadcast_add_fusion.1, bf16[24,32,384]{2,1,0:T(8,128)(2,1)} %param.9, bf16[24,32,384]{2,1,0:T(8,128)(2,1)} %param.7), kind=kLoop, calls=%fused_computation.1 | loop fusion | flops 884736 | bytes 3543552 | tf_op jit(solution)/shard_map/jit(_where)/select_n | solution.py:19
  4.6 0.9 copy.16
  5.5 5.3 %reshape.77 = bf16[24,32,16,24]{3,2,1,0:T(8,128)(2,1)S(1)} reshape(bf16[24,32,384]{2,1,0:T(8,128)(2,1)} %copy.16) | data formatting | bytes 1179648 | tf_op jit(solution)/shard_map/reshape | solution.py:294
  10.8 3.6 %copy.17 = bf16[16,24,24,32]{3,2,1,0:T(8,128)(2,1)} copy(bf16[16,24,24,32]{2,0,3,1:T(8,128)(2,1)S(1)} %bitcast.12) | data formatting | bytes 1179648 | tf_op jit(solution)/shard_map/transpose | solution.py:294
  14.4 4.0 %reshape.78.upper_ref = bf16[16,24,768]{2,1,0:T(8,128)(2,1)} reshape(bf16[16,24,24,32]{3,2,1,0:T(8,128)(2,1)} %copy.17) | data formatting | bytes 1179648 | tf_op jit(solution)/shard_map/reshape | solution.py:294
  18.4 0.0 copy-start
  18.4 2.9 %copy.18 = bf16[1024,1024]{0,1:T(8,128)(2,1)S(1)} copy(bf16[1024,1024]{1,0:T(8,128)(2,1)} %param.10) | data formatting | bytes 4194304 | tf_op args[3]
  21.3 0.0 copy-done
  21.3 0.1 broadcast_add_fusion
  21.4 0.1 add.59
  21.4 0.5 compare_select_fusion
  22.0 2.5 %copy.19 = bf16[32,32,1024]{2,1,0:T(8,128)(2,1)} copy(bf16[32,32,1024]{2,0,1:T(8,128)(2,1)S(1)} %bitcast.14) | data formatting | bytes 4194304 | tf_op jit(solution)/shard_map/transpose | solution.py:297
  24.5 157.6 %edge_update.1 = bf16[768,384]{1,0:T(8,128)(2,1)} custom-call(bf16[32,24,384]{2,1,0:T(8,128)(2,1)} %get-tuple-element.7.edge_ref, bf16[32,24,384]{2,1,0:T(8,128)(2,1)} %get-tuple-element.6.lower_ref, bf16[16,24,768]{2,1,0:T(8,128)(2,1)} %reshape.78.upper_ref, bf16[1024,1024]{1,0:T(8,128)(2,1)} %bitcast.13), custom_call_target="tpu_custom_call" | custom-call | tf_op jit(solution)/shard_map/edge_update/pallas_call | solution.py:302
  182.1 1.9 %copy.24 = bf16[24,32,384]{2,1,0:T(8,128)(2,1)} copy(bf16[24,32,384]{2,1,0:T(8,128)(2,1)} %bitcast.15) | data formatting | bytes 1179648
Async XLA Ops:
  18.4 2.9 %copy-start = (s32[32]{0:T(128)S(1)}, s32[32]{0:T(128)}, u32[]{:S(2)}) copy-start(s32[32]{0:T(128)} %param.12) | copy-start | bytes 388

commit v2 on v1

v2 whole, which is shorter than its diff:
```python
import functools

import jax
import jax.numpy as jnp
from jax import lax
from jax.experimental import pallas as pl
from jax.experimental.pallas import tpu as pltpu
from jax.sharding import PartitionSpec as P

BF = jnp.bfloat16
F32 = jnp.float32
LANES = 128
GROUP = 4
CUTS = 2
EDGE, LOWER = 0, 1
RIGHT, LEFT, ACROSS, SIBLING = 0, 1, 2, 3
MESH = pl.DeviceIdType.MESH


def masked_rows(piece, charges, bond_charge, new_charge):
    keep = charges[:, None, None] + bond_charge[None, :, None] == new_charge[None, None, :]
    return jnp.where(keep, piece, jnp.zeros_like(piece))


def plain(edge, proj_upper, proj_lower, site, chi_charge, bond_charge, new_charge):
    rows = edge.shape[0]
    kdim = bond_charge.shape[0]
    width = chi_charge.shape[0]
    mine = lax.axis_index("chi") * rows
    pair = (bond_charge[:, None] + bond_charge[None, :]).reshape(kdim * kdim)
    block = jnp.where(pair[:, None] == pair[None, :], site, jnp.zeros_like(site))
    piece = lax.all_gather(proj_upper, "chi", axis=0, tiled=True)
    count = piece.shape[0]
    masked = masked_rows(piece, chi_charge, bond_charge, new_charge)
    half = jnp.dot(
        edge.reshape(rows * kdim, count),
        masked.reshape(count, kdim * width),
        preferred_element_type=F32,
    )
    half = half.astype(BF).reshape(rows, kdim * kdim, width)
    grown = jnp.einsum("bxc,xy->byc", half, block, preferred_element_type=F32).astype(BF)
    grown = grown.reshape(rows, kdim, kdim, width)
    own_charges = lax.dynamic_slice_in_dim(chi_charge, mine, rows)
    lower = masked_rows(proj_lower, own_charges, bond_charge, new_charge)
    raw = lax.psum_scatter(
        jnp.einsum("brdc,bde->cre", grown, lower, preferred_element_type=F32),
        "chi",
        scatter_dimension=0,
        tiled=True,
    )
    largest = lax.pmax(jnp.max(jnp.abs(raw)), "chi")
    return (raw / (largest + 1e-06)).astype(BF)


def kernel(
    n, depth, edge_ref, lower_ref, upper_ref, block_ref, own_ref, chip_ref, new_ref, bond_ref, out_ref,
    edge_all, lower_all, swap, up_tx, up_rx, up_wide, up_t, state, total, peaks,
    swap_send, swap_recv, up_send, up_recv, blk_send, blk_recv, peak_send, peak_recv,
):
    kdim, rows, width = edge_ref.shape
    part = kdim // 2
    wide = 2 * rows
    chips = n // 2
    pairs = kdim * kdim
    me = lax.axis_index("chi")
    core = lax.rem(me, 2)
    chip = me // 2
    y = lax.rem(chip, 2)
    z = chip // 2
    sibling = me + 1 - 2 * core

    barrier = pltpu.get_barrier_semaphore()

    def greet(j, carry):
        pl.semaphore_signal(barrier, inc=1, device_id={"chi": lax.rem(me + j, n)}, device_id_type=MESH)
        return carry

    lax.fori_loop(1, n, greet, 0)
    pl.semaphore_wait(barrier, n - 1)

    ins = (edge_ref, lower_ref)
    fulls = (edge_all, lower_all)

    def swap_copy(which):
        return pltpu.make_async_remote_copy(
            src_ref=ins[which].at[pl.ds(part * (1 - core), part)],
            dst_ref=swap.at[which],
            send_sem=swap_send.at[which],
            recv_sem=swap_recv.at[which],
            device_id={"chi": sibling},
            device_id_type=MESH,
        )

    def slot_of(q, at):
        qz, az = q // 2, at // 2
        gap = jnp.abs(qz - az)
        rank = jnp.int32(0)
        for other in range(depth):
            far = jnp.abs(other - az)
            nearer = jnp.logical_or(far < gap, jnp.logical_and(far == gap, other < qz))
            rank = rank + nearer.astype(jnp.int32)
        return 2 * rank + lax.rem(q + at, 2)

    piece = part // CUTS

    def block_copy(which, q, side, way, target, cut):
        here, there = slot_of(q, chip), slot_of(q, target // 2)
        return pltpu.make_async_remote_copy(
            src_ref=fulls[which].at[here, pl.ds(part * side + piece * cut, piece)],
            dst_ref=fulls[which].at[there, pl.ds(part * side + piece * cut, piece)],
            send_sem=blk_send.at[which, q, way, cut],
            recv_sem=blk_recv.at[which, there, side, cut],
            device_id={"chi": target},
            device_id_type=MESH,
        )

    def ways(which, q, cut):
        targets = (me + 4, me - 4, me + 2 - 4 * y, sibling)

        def send(way):
            block_copy(which, q, core, way, targets[way], cut).start()

        def leave(way):
            block_copy(which, q, core, way, targets[way], cut).wait_send()

        return send, leave

    def arrived(which, q, side, cut):
        block_copy(which, q, side, SIBLING, sibling, cut).wait_recv()

    def whole(which, lo, hi):
        def wait(slot):
            for cut in range(CUTS):
                here = fulls[which].at[slot, pl.ds(part * (1 - core) + piece * cut, piece)]
                pltpu.make_async_remote_copy(
                    src_ref=here, dst_ref=here, send_sem=blk_send.at[which, 0, SIBLING, cut],
                    recv_sem=blk_recv.at[which, slot, 1 - core, cut],
                    device_id={"chi": sibling}, device_id_type=MESH,
                ).wait_recv()

        each(lo, hi, wait)

    def up_copy(j):
        to = lax.rem(me + j, n)
        return pltpu.make_async_remote_copy(
            src_ref=up_tx.at[to],
            dst_ref=up_rx.at[me],
            send_sem=up_send.at[j],
            recv_sem=up_recv.at[j],
            device_id={"chi": to},
            device_id_type=MESH,
        )

    def each(lo, hi, act):
        def body(j, carry):
            act(j)
            return carry

        lax.fori_loop(lo, hi, body, 0)

    def join(which):
        swap_copy(which).wait_recv()

        def body(j):
            own = ins[which][part * core + j].astype(F32)
            other = swap[which, j].astype(F32)
            first = jnp.where(core == 0, own, other)
            second = jnp.where(core == 0, other, own)
            both = jnp.concatenate([first, second], axis=0)
            if which == LOWER:
                keep = chip_ref[...] + bond_ref[part * core + j] == new_ref[...]
                both = jnp.where(keep, both, jnp.zeros_like(both))
            fulls[which][0, part * core + j] = both.astype(BF)

        each(0, part, body)

    beyond = chip + 1 - 2 * y

    def open_across(which):
        for cut in range(CUTS):
            send, _ = ways(which, chip, cut)
            send(ACROSS)
            send(SIBLING)

    def open_line(which):
        for cut in range(CUTS):
            send, _ = ways(which, chip, cut)
            pl.when(z < depth - 1)(lambda: send(RIGHT))
            pl.when(z > 0)(lambda: send(LEFT))

    def along(which, s):
        for cut in range(CUTS):
            @pl.when(z - s >= 0)
            def _():
                q = chip - 2 * s
                arrived(which, q, core, cut)
                send, _ = ways(which, q, cut)
                pl.when(z < depth - 1)(lambda: send(RIGHT))
                send(ACROSS)
                send(SIBLING)

            @pl.when(z + s < depth)
            def _():
                q = chip + 2 * s
                arrived(which, q, core, cut)
                send, _ = ways(which, q, cut)
                pl.when(z > 0)(lambda: send(LEFT))
                send(ACROSS)
                send(SIBLING)

    def beside(which, s):
        for cut in range(CUTS):
            for sign in (-1, 1) if s else (1,):
                @pl.when(jnp.logical_and(z + sign * s >= 0, z + sign * s < depth))
                def _():
                    q = beyond + 2 * sign * s
                    arrived(which, q, core, cut)
                    block_copy(which, q, core, SIBLING, sibling, cut).start()

    def sent(which):
        def body(q):
            column = q // 2
            mine = lax.rem(q, 2) == y
            for cut in range(CUTS):
                _, leave = ways(which, q, cut)
                pl.when(jnp.logical_and(mine, jnp.logical_and(column <= z, z < depth - 1)))(lambda: leave(RIGHT))
                pl.when(jnp.logical_and(mine, jnp.logical_and(column >= z, z > 0)))(lambda: leave(LEFT))
                pl.when(mine)(lambda: leave(ACROSS))
                leave(SIBLING)

        each(0, chips, body)

    def rows_of(full, t, j):
        lo, hi = LANES * t, LANES * (t + 1)
        cuts = []
        for slot in range(lo // wide, (hi + wide - 1) // wide):
            start, stop = max(lo - slot * wide, 0), min(hi - slot * wide, wide)
            cuts.append(full[slot, j, start:stop, :])
        return cuts

    def first(t, lo, hi):
        def body(j):
            right = jnp.concatenate(rows_of(edge_all, t, 2 * j) + rows_of(edge_all, t, 2 * j + 1), axis=0)
            half = lax.dot_general(up_t[...], right, (((1,), (1,)), ((), ())), preferred_element_type=F32)
            half = half.astype(BF)
            at = pl.multiple_of(2 * j * kdim, 2 * kdim)
            state[t, 1:rows + 1, pl.ds(at, kdim), :] = half[:, :LANES].reshape(rows, kdim, LANES)
            state[t, 1:rows + 1, pl.ds(at + kdim, kdim), :] = half[:, LANES:].reshape(rows, kdim, LANES)

        each(lo, hi, body)

    def second(t, lo, hi):
        def body(j):
            c = GROUP * j
            right = jnp.concatenate([state[t, c + 1 + i] for i in range(GROUP)], axis=1)
            grown = jnp.dot(block_ref[...], right, preferred_element_type=F32).astype(BF)
            for i in range(GROUP):
                state[t, c + i] = grown[:, i * LANES:(i + 1) * LANES]

        each(lo, hi, body)

    def third(t):
        def body(j):
            lefts, rights = [], []
            for i in range(4):
                at = pl.multiple_of((4 * j + i) * kdim, kdim)
                lefts.append(state[t, 0:rows, pl.ds(at, kdim), :].reshape(rows * kdim, LANES))
                rights += rows_of(lower_all, t, 4 * j + i)
            total[...] += jnp.dot(
                jnp.concatenate(lefts, axis=1), jnp.concatenate(rights, axis=0), preferred_element_type=F32
            )

        each(0, kdim // 4, body)

    steps = rows // GROUP
    swap_copy(EDGE).start()
    swap_copy(LOWER).start()
    join(EDGE)
    open_line(EDGE)
    open_across(EDGE)
    upper = jnp.where(own_ref[...] == new_ref[...], upper_ref[...].astype(F32), 0.0).T
    for j in range(n):
        up_tx[j] = upper[j * rows:(j + 1) * rows, :].astype(BF)
    each(1, n, lambda j: up_copy(j).start())
    join(LOWER)
    up_rx[me] = up_tx[me]
    total[...] = jnp.zeros_like(total)
    beside(EDGE, 0)
    along(EDGE, 1)
    each(1, n, lambda j: up_copy(j).wait_recv())
    up_wide[...] = up_rx[...].astype(F32)
    lane = lax.broadcasted_iota(jnp.int32, (n, width), 1)
    sender = lax.broadcasted_iota(jnp.int32, (n, width), 0)
    spread = jnp.logical_and(lane >= sender * rows, lane < (sender + 1) * rows).astype(F32).astype(BF)
    within = lax.rem(lax.broadcasted_iota(jnp.int32, (rows, 1, width), 2), rows)
    chosen = within == lax.broadcasted_iota(jnp.int32, (rows, 1, width), 0)
    for c in range(rows):
        spots = lax.dot_general(
            up_wide[:, c, :].astype(BF), spread, (((0,), (0,)), ((), ())), preferred_element_type=F32
        ).reshape(rows, kdim, width)
        up_t[c * kdim:(c + 1) * kdim, :] = jnp.sum(jnp.where(chosen, spots, 0.0), axis=0).astype(BF)
    beside(EDGE, 1)
    along(EDGE, 2)
    whole(EDGE, 0, 3)
    first(0, 0, kdim // 2)
    beside(EDGE, 2)
    along(EDGE, 3)
    open_line(LOWER)
    open_across(LOWER)
    second(0, 0, steps)
    beside(EDGE, 3)
    whole(EDGE, 3, 6)
    first(1, 0, kdim // 2)
    beside(LOWER, 0)
    along(LOWER, 1)
    whole(EDGE, 6, chips)
    first(2, 0, kdim // 2)
    second(1, 0, steps // 2)
    beside(LOWER, 1)
    along(LOWER, 2)
    second(1, steps // 2, steps)
    second(2, 0, steps // 2)
    beside(LOWER, 2)
    along(LOWER, 3)
    second(2, steps // 2, steps)
    whole(LOWER, 0, 3)
    third(0)
    whole(LOWER, 3, 6)
    third(1)
    beside(LOWER, 3)
    whole(LOWER, 6, chips)
    third(2)

    peaks[me] = jnp.full(peaks.shape[1:], jnp.max(jnp.abs(total[...])), F32)

    def peak_copy(j):
        return pltpu.make_async_remote_copy(
            src_ref=peaks.at[me],
            dst_ref=peaks.at[me],
            send_sem=peak_send.at[j],
            recv_sem=peak_recv.at[j],
            device_id={"chi": lax.rem(me + j, n)},
            device_id_type=MESH,
        )

    each(1, n, lambda j: peak_copy(j).start())
    each(0, 2, lambda w: pltpu.make_async_remote_copy(
        src_ref=edge_ref.at[pl.ds(0, part)], dst_ref=swap.at[w], send_sem=swap_send.at[w],
        recv_sem=swap_recv.at[w], device_id={"chi": sibling}, device_id_type=MESH).wait_send())
    each(1, n, lambda j: up_copy(j).wait_send())
    sent(EDGE)
    sent(LOWER)
    each(1, n, lambda j: peak_copy(j).wait_recv())
    each(1, n, lambda j: peak_copy(j).wait_send())
    largest = jnp.max(peaks[...])
    out_ref[...] = (total[...] / (largest + 1e-06)).astype(BF)


def fused(n, edge, proj_upper, proj_lower, site, chi_charge, bond_charge, new_charge):
    rows, kdim, width = edge.shape
    mine = lax.axis_index("chi") * rows
    own = lax.dynamic_slice_in_dim(chi_charge, mine, rows)
    own = (own[:, None] + bond_charge[None, :]).reshape(rows * kdim, 1)
    start = lax.axis_index("chi") // 2 * (2 * rows)
    chip = lax.dynamic_slice_in_dim(chi_charge, start, 2 * rows)[:, None]
    pair = (bond_charge[:, None] + bond_charge[None, :]).reshape(kdim * kdim)
    block = jnp.where(pair[:, None] == pair[None, :], site, jnp.zeros_like(site))
    block = block.reshape(kdim * kdim, kdim, kdim).transpose(2, 1, 0).reshape(kdim * kdim, kdim * kdim)
    chips = n // 2
    part = kdim // 2
    dma = pltpu.SemaphoreType.DMA
    vmem = pl.BlockSpec(memory_space=pltpu.VMEM)
    out = pl.pallas_call(
        functools.partial(kernel, n, chips // 2),
        out_shape=jax.ShapeDtypeStruct((rows * kdim, width), BF),
        in_specs=[vmem] * 7 + [pl.BlockSpec(memory_space=pltpu.SMEM)],
        out_specs=vmem,
        scratch_shapes=[
            pltpu.VMEM((chips, kdim, 2 * rows, width), BF),
            pltpu.VMEM((chips, kdim, 2 * rows, width), BF),
            pltpu.VMEM((2, part, rows, width), BF),
            pltpu.VMEM((n, rows, rows * kdim), BF),
            pltpu.VMEM((n, rows, rows * kdim), BF),
            pltpu.VMEM((n, rows, rows * kdim), F32),
            pltpu.VMEM((rows * kdim, width), BF),
            pltpu.VMEM((width // LANES, rows + 1, kdim * kdim, LANES), BF),
            pltpu.VMEM((rows * kdim, width), F32),
            pltpu.VMEM((n, 8, 128), F32),
            dma((2,)), dma((2,)),
            dma((n,)), dma((n,)),
            dma((2, chips, 4, CUTS)), dma((2, chips, 2, CUTS)),
            dma((n,)), dma((n,)),
        ],
        compiler_params=pltpu.CompilerParams(
            collective_id=0, has_side_effects=True, vmem_limit_bytes=63 * 1024 * 1024
        ),
        name="edge_update",
    )(
        edge.transpose(1, 0, 2), proj_lower.transpose(1, 0, 2), proj_upper.reshape(rows * kdim, width), block,
        own, chip, new_charge[None, :], bond_charge,
    )
    return out.reshape(rows, kdim, width)


def solution(mesh):
    n = mesh.shape["chi"]

    def local(edge, *rest):
        rows, kdim, width = edge.shape
        if n == 16 and rows % 8 == 0 and rows % 6 == 0 and kdim % 32 == 0 and width == 3 * LANES:
            return fused(n, edge, *rest)
        return plain(edge, *rest)

    placed = (
        P(("grp", "chi"), None, None),
        P(("grp", "chi"), None, None),
        P(("grp", "chi"), None, None),
        P("grp", None),
        P("grp"),
        P("grp"),
        P("grp"),
    )
    return jax.shard_map(
        local, mesh=mesh, in_specs=placed, out_specs=P(("grp", "chi"), None, None), check_vma=False
    )
```

time: 184 us -> 163 us (0.89)
  local copies, waits for them, and re-layouts: 21.9 us -> 12.6 us
  Pallas kernels: 158 us -> 149 us
  other arithmetic: 4.42 us -> 0.69 us
    reshape x2 -> x0, local copies, waits for them, and re-layouts: 9.33 us -> none  [fused(): upper.reshape(rows, kdim, n, rows).transpose(2, 0, 3, 1)]
    pallas_call x1, Pallas kernels: 158 us -> 149 us  [fused(): pl.pallas_call(functools.partial(kernel, n, chips // 2), out_shape=jax.Sh...]
    select_n x1 -> x0, other arithmetic: 3.08 us -> none  [masked_rows(): return jnp.where(keep, piece, jnp.zeros_like(piece))]
    unnamed x4 -> x8, local copies, waits for them, and re-layouts: 4.81 us -> 4.82 us
where the time goes in v2:
time: 163 us
  Pallas kernels  149 us (91%)
  local copies, waits for them, and re-layouts  12.6 us (8%)
    pallas_call x1, Pallas kernels, fused(): pl.pallas_call(functools.partial(kernel, n, chips // 2), out_shape=jax.Sh...  149 us
    unnamed x8, local copies, waits for them, and re-layouts  4.82 us

profile of v2, /device:TPU:0, one launch (start us, length us, event | category | flops | bytes accessed | tf_op | source)
XLA Modules:
  0.0 162.7 jit_solution(8552025557378703027)
XLA Ops:
  0.0 2.6 %copy_bitcast_fusion = (bf16[32,24,384]{2,1,0:T(8,128)(2,1)}, bf16[32,24,384]{2,1,0:T(8,128)(2,1)}) fusion(bf16[24,32,384]{2,1,0:T(8,128)(2,1)} %param.9, bf16[24,32,384]{2,1,0:T(8,128)(2,1)} %param.7), kind=kLoop, calls=%fused_computation.1 | loop fusion | bytes 2359296 | tf_op jit(solution)/shard_map/transpose | solution.py:399
  2.7 0.0 copy-start
  2.7 2.9 %copy.14 = bf16[1024,1024]{0,1:T(8,128)(2,1)S(1)} copy(bf16[1024,1024]{1,0:T(8,128)(2,1)} %param.10) | data formatting | bytes 4194304 | tf_op args[3]
  5.5 0.0 copy-done
  5.5 0.1 broadcast_add_fusion
  5.6 0.1 add.57
  5.7 0.5 compare_select_fusion
  6.2 0.0 copy-start.2
  6.2 0.0 copy-start.1
  6.3 2.5 %copy.15 = bf16[32,32,1024]{2,1,0:T(8,128)(2,1)} copy(bf16[32,32,1024]{2,0,1:T(8,128)(2,1)S(1)} %bitcast.13) | data formatting | bytes 4194304 | tf_op jit(solution)/shard_map/transpose | solution.py:368
  8.7 0.0 copy-done.2
  8.7 0.1 dynamic_slice.6
  8.8 0.1 broadcast_add_fusion.1
  8.9 1.1 add.64.own_ref
  10.0 0.1 dynamic-slice_bitcast_fusion
  10.1 0.7 copy.17.chip_ref
  10.8 0.0 copy-done.1
  10.8 0.6 broadcast_in_dim.15.new_ref
  11.4 149.4 %edge_update.1 = bf16[768,384]{1,0:T(8,128)(2,1)} custom-call(bf16[32,24,384]{2,1,0:T(8,128)(2,1)} %get-tuple-element.6.edge_ref, bf16[32,24,384]{2,1,0:T(8,128)(2,1)} %get-tuple-element.5.lower_ref, bf16[768,384]{1,0:T(8,128)(2,1)} %bitcast.15, bf16[1024,1024]{1,0:T(8,128)(2,1)} %bitcast.12, s32[768,1]{1,0:T(8,128)} %add.64.own_ref, ...), custom_call_target="tpu_custom_call" | custom-call | tf_op jit(solution)/shard_map/edge_update/pallas_call | solution.py:373
  160.8 1.9 %copy.21 = bf16[24,32,384]{2,1,0:T(8,128)(2,1)} copy(bf16[24,32,384]{2,1,0:T(8,128)(2,1)} %bitcast.14) | data formatting | bytes 1179648
Async XLA Ops:
  2.7 2.9 %copy-start = (s32[32]{0:T(128)S(1)}, s32[32]{0:T(128)}, u32[]{:S(2)}) copy-start(s32[32]{0:T(128)} %bond_ref.1) | copy-start | bytes 388
  6.2 2.5 %copy-start.2 = (s32[384]{0:T(512)S(1)}, s32[384]{0:T(512)}, u32[]{:S(2)}) copy-start(s32[384]{0:T(512)} %param.11) | copy-start | bytes 4612
  6.2 4.6 %copy-start.1 = (s32[384]{0:T(512)S(1)}, s32[384]{0:T(512)}, u32[]{:S(2)}) copy-start(s32[384]{0:T(512)} %param.13) | copy-start | bytes 4612

commit v3 on v2

--- a/solution.py
+++ b/solution.py
@@ -53,8 +53,8 @@
 
 
 def kernel(
-    n, depth, edge_ref, lower_ref, upper_ref, block_ref, own_ref, chip_ref, new_ref, bond_ref, out_ref,
-    edge_all, lower_all, swap, up_tx, up_rx, up_wide, up_t, state, total, peaks,
+    n, depth, edge_ref, lower_ref, upper_ref, site_ref, own_ref, chip_ref, new_ref, pair_ref, column_ref, bond_ref, out_ref,
+    edge_all, lower_all, swap, up_tx, up_rx, up_wide, up_t, turned, block_ref, state, total, peaks,
     swap_send, swap_recv, up_send, up_recv, blk_send, blk_recv, peak_send, peak_recv,
 ):
     kdim, rows, width = edge_ref.shape
@@ -287,6 +287,17 @@
     total[...] = jnp.zeros_like(total)
     beside(EDGE, 0)
     along(EDGE, 1)
+    for i in range(pairs // LANES):
+        turned[i] = site_ref[i * LANES:(i + 1) * LANES, :].astype(F32).T
+    for d in range(kdim):
+        keep = column_ref[...] + bond_ref[d] == pair_ref[...]
+        block_ref[d * kdim:(d + 1) * kdim, :] = jnp.where(
+            keep,
+            jnp.concatenate(
+                [turned[i, pl.ds(d, kdim, stride=kdim), :] for i in range(pairs // LANES)], axis=1
+            ),
+            0.0,
+        ).astype(BF)
     each(1, n, lambda j: up_copy(j).wait_recv())
     up_wide[...] = up_rx[...].astype(F32)
     lane = lax.broadcasted_iota(jnp.int32, (n, width), 1)
@@ -364,8 +375,6 @@
     start = lax.axis_index("chi") // 2 * (2 * rows)
     chip = lax.dynamic_slice_in_dim(chi_charge, start, 2 * rows)[:, None]
     pair = (bond_charge[:, None] + bond_charge[None, :]).reshape(kdim * kdim)
-    block = jnp.where(pair[:, None] == pair[None, :], site, jnp.zeros_like(site))
-    block = block.reshape(kdim * kdim, kdim, kdim).transpose(2, 1, 0).reshape(kdim * kdim, kdim * kdim)
     chips = n // 2
     part = kdim // 2
     dma = pltpu.SemaphoreType.DMA
@@ -373,7 +382,7 @@
     out = pl.pallas_call(
         functools.partial(kernel, n, chips // 2),
         out_shape=jax.ShapeDtypeStruct((rows * kdim, width), BF),
-        in_specs=[vmem] * 7 + [pl.BlockSpec(memory_space=pltpu.SMEM)],
+        in_specs=[vmem] * 9 + [pl.BlockSpec(memory_space=pltpu.SMEM)],
         out_specs=vmem,
         scratch_shapes=[
             pltpu.VMEM((chips, kdim, 2 * rows, width), BF),
@@ -383,6 +392,8 @@
             pltpu.VMEM((n, rows, rows * kdim), BF),
             pltpu.VMEM((n, rows, rows * kdim), F32),
             pltpu.VMEM((rows * kdim, width), BF),
+            pltpu.VMEM((kdim * kdim // LANES, kdim * kdim, LANES), F32),
+            pltpu.VMEM((kdim * kdim, kdim * kdim), BF),
             pltpu.VMEM((width // LANES, rows + 1, kdim * kdim, LANES), BF),
             pltpu.VMEM((rows * kdim, width), F32),
             pltpu.VMEM((n, 8, 128), F32),
@@ -396,8 +407,8 @@
         ),
         name="edge_update",
     )(
-        edge.transpose(1, 0, 2), proj_lower.transpose(1, 0, 2), proj_upper.reshape(rows * kdim, width), block,
-        own, chip, new_charge[None, :], bond_charge,
+        edge.transpose(1, 0, 2), proj_lower.transpose(1, 0, 2), proj_upper.reshape(rows * kdim, width), site,
+        own, chip, new_charge[None, :], pair[None, :], bond_charge[:, None], bond_charge,
     )
     return out.reshape(rows, kdim, width)
 

time: 163 us -> 162 us (level)
    unnamed x8 -> x1, local copies, waits for them, and re-layouts: 4.82 us -> 1.94 us
    transpose x1 -> x0, local copies, waits for them, and re-layouts: 2.48 us -> none  [fused(): block.reshape(kdim * kdim, kdim, kdim).transpose(2, 1, 0)]
where the time goes in v3:
time: 162 us
  Pallas kernels  149 us (92%)
  local copies, waits for them, and re-layouts  11.2 us (7%)
    pallas_call x1, Pallas kernels, fused(): pl.pallas_call(functools.partial(kernel, n, chips // 2), out_shape=jax.Sh...  149 us

profile of v3, /device:TPU:0, one launch (start us, length us, event | category | flops | bytes accessed | tf_op | source)
XLA Modules:
  0.0 162.1 jit_solution(590922427152074775)
XLA Ops:
  0.0 0.8 dynamic-slice_bitcast_fusion
  0.8 0.8 dynamic_slice.6
  1.5 1.3 broadcast_in_dim.14.new_ref
  2.8 0.7 broadcast_add_fusion.1
  3.5 1.3 copy.16.column_ref
  4.8 0.8 broadcast_add_fusion
  5.6 0.7 add.62.pair_ref
  6.3 0.7 copy.15.chip_ref
  7.0 1.2 add.63.own_ref
  8.2 2.6 %copy_bitcast_fusion = (bf16[32,24,384]{2,1,0:T(8,128)(2,1)}, bf16[32,24,384]{2,1,0:T(8,128)(2,1)}) fusion(bf16[24,32,384]{2,1,0:T(8,128)(2,1)} %param.9, bf16[24,32,384]{2,1,0:T(8,128)(2,1)} %param.7), kind=kLoop, calls=%fused_computation | loop fusion | bytes 2359296 | tf_op jit(solution)/shard_map/transpose | solution.py:410
  10.8 149.4 %edge_update.1 = bf16[768,384]{1,0:T(8,128)(2,1)} custom-call(bf16[32,24,384]{2,1,0:T(8,128)(2,1)} %get-tuple-element.6.edge_ref, bf16[32,24,384]{2,1,0:T(8,128)(2,1)} %get-tuple-element.5.lower_ref, bf16[768,384]{1,0:T(8,128)(2,1)} %bitcast.10, bf16[1024,1024]{1,0:T(8,128)(2,1)} %site_ref.1, s32[768,1]{1,0:T(8,128)} %add.63.own_ref, ...), custom_call_target="tpu_custom_call" | custom-call | tf_op jit(solution)/shard_map/edge_update/pallas_call | solution.py:382
  160.2 1.9 %copy.20 = bf16[24,32,384]{2,1,0:T(8,128)(2,1)} copy(bf16[24,32,384]{2,1,0:T(8,128)(2,1)} %bitcast.9) | data formatting | bytes 1179648
